TPU v7x, 32 devices: a whole 2x2x4 slice. The times are simulated.
32 devices in a mesh: dp: 2 (over x), expert: 4 (over y, core), mp: 4 (over z).
Axes of the slice: x: 2, y: 2, z: 4, core: 2. Of those that a mesh axis runs over, the one named last changes fastest.
Arguments:
- tokens: bfloat16 [128, 3072], P('dp'), may hold values from -6 to 6
- expert_ids: int32 [128, 2], P('dp'), may hold values from 0 to 3, all different within a row; in each aligned block of 64 rows (0 to 63, 64 to 127, ...) at most 64 rows name the same one
- gate_values: float32 [128, 2], P('dp'), may hold values from 0.2 to 1
- targets: int32 [128], P('dp'), may hold values from 0 to 32767
- w_gate: bfloat16 [4, 3072, 4, 2048], P('expert', None, 'mp', 'dp'), may hold values from -0.109375 to 0.109375
- w_up: bfloat16 [4, 3072, 4, 2048], P('expert', None, 'mp', 'dp'), may hold values from -0.109375 to 0.109375
- w_down: bfloat16 [4, 4, 2048, 3072], P('expert', 'mp', None, 'dp'), may hold values from -0.0625 to 0.0625
- norm_gain: float32 [3072], replicated, may hold values from 0.1 to 1.9
- lens_head: bfloat16 [3072, 32768], P('dp', ('expert', 'mp')), may hold values from -120 to 120
Outputs:
- mixed: bfloat16 [128, 3072], P('dp')
- log_probs: float32 [128], P('dp')
Inputs may be any that keep to these rules, and one draw needn't show every extreme that they name: `expert_ids`: each row names two different experts; in each aligned block of 64 rows no expert is named by more than 64 rows, a bound that some block reaches.
All inputs are finite; a program needn't handle non-finite values.
Results may differ from a plain program's by a relative error of at most 0.0041.
Values may be sent and summed in bfloat16 or wider, within the bound.
A program may use at most 128 MiB of HBM per device.

v0:
```python
import jax
import jax.numpy as jnp
from jax import lax
from jax.sharding import PartitionSpec as P

f32, bf16 = (jnp.float32, jnp.bfloat16)


def per_device(
    tokens, expert_ids, gate_values, targets, w_gate, w_up, w_down, norm_gain, lens_head
):
    rows, feats = tokens.shape
    owner = lax.axis_index("expert")
    weights = jnp.sum(jnp.where(expert_ids == owner, gate_values, f32(0.0)), axis=1)
    gate_mat = w_gate.reshape(feats, -1)
    up_mat = w_up.reshape(feats, -1)
    down_mat = w_down.reshape(w_down.shape[2], w_down.shape[3])
    own_feats = down_mat.shape[1]
    all_tokens = lax.all_gather(tokens, "dp", axis=0, tiled=True)
    all_weights = lax.all_gather(weights, "dp", axis=0, tiled=True)
    gate_part = jnp.dot(all_tokens, gate_mat, preferred_element_type=f32)
    up_part = jnp.dot(all_tokens, up_mat, preferred_element_type=f32)
    hidden = (jax.nn.silu(gate_part) * up_part).astype(bf16)
    hidden = lax.all_gather(hidden, "dp", axis=1, tiled=True)
    part = jnp.dot(hidden, down_mat, preferred_element_type=f32) * all_weights[:, None]
    summed = lax.psum(part, ("expert", "mp"))
    first = lax.axis_index("dp") * own_feats
    own_tokens = lax.dynamic_slice_in_dim(all_tokens, first, own_feats, axis=1)
    own_gain = lax.dynamic_slice_in_dim(norm_gain, first, own_feats, axis=0)
    mixed_part = (own_tokens.astype(f32) + summed).astype(bf16)
    mixed = lax.all_to_all(mixed_part, "dp", split_axis=0, concat_axis=1, tiled=True)
    mixed_f = mixed.astype(f32)
    scale = lax.rsqrt(jnp.mean(mixed_f * mixed_f, axis=1) + 1e-05)
    gained = (mixed_part.astype(f32) * own_gain[None, :]).astype(bf16)
    logits_part = jnp.dot(gained, lens_head, preferred_element_type=f32)
    logits = lax.psum_scatter(logits_part, "dp", scatter_dimension=0, tiled=True)
    logits = logits * scale[:, None]
    vocab_cols = lens_head.shape[1]
    vocab_start = (owner * lax.axis_size("mp") + lax.axis_index("mp")) * vocab_cols
    columns = vocab_start + lax.broadcasted_iota(jnp.int32, (1, vocab_cols), 1)
    hit = columns == targets[:, None]
    target_local = jnp.sum(jnp.where(hit, logits, f32(0.0)), axis=1)
    top = jnp.max(logits, axis=1)
    total = jnp.sum(jnp.exp(logits - top[:, None]), axis=1)
    stats = lax.all_gather(jnp.stack([top, total, target_local]), ("expert", "mp"))
    tops, totals, hits = (stats[:, 0], stats[:, 1], stats[:, 2])
    top_all = jnp.max(tops, axis=0)
    exp_total = jnp.sum(totals * jnp.exp(tops - top_all[None, :]), axis=0)
    log_probs = jnp.sum(hits, axis=0) - top_all - jnp.log(exp_total)
    return (mixed, log_probs)


def solution(mesh):
    in_specs = (
        P("dp", None),
        P("dp", None),
        P("dp", None),
        P("dp"),
        P("expert", None, "mp", "dp"),
        P("expert", None, "mp", "dp"),
        P("expert", "mp", None, "dp"),
        P(),
        P("dp", ("expert", "mp")),
    )
    out_specs = (P("dp", None), P("dp"))
    return jax.shard_map(
        per_device, mesh=mesh, in_specs=in_specs, out_specs=out_specs, check_vma=False
    )
```

profile of v0, /device:TPU:0, one launch (start us, length us, event | category | flops | bytes accessed | tf_op | source)
XLA Modules:
  0.0 207.5 jit_solution(1650163457520954662)
XLA Ops:
  7.2 0.0 all-reduce.3.cloned.1.call-start
  7.2 0.0 slice-start
  7.2 13.1 %all_gather.15 = bf16[128,3072]{1,0:T(8,128)(2,1)S(1)} all-gather(bf16[64,3072]{1,0:T(8,128)(2,1)} %param.9), channel_id=1, replica_groups=mesh['dp'=2,'expert'=4,'mp'=4] {'dp'}, dimensions={0}, use_global_device_ids=true | all-gather | bytes 1179648 | tf_op jit(solution)/shard_map/all_gather | solution.py:19
  20.3 3.9 %fusion.4 = f32[128,1024]{1,0:T(8,128)S(1)} fusion(bf16[128,3072]{1,0:T(8,128)(2,1)S(1)} %all_gather.15, bf16[1,3072,1,1024]{3,1,2,0:T(8,128)(2,1)} %param.13), kind=kOutput, calls=%fused_computation.4 | convolution fusion | flops 805306368 | bytes 7602176 | tf_op jit(solution)/shard_map/dot_general | solution.py:21
  24.2 0.0 slice-done
  24.2 0.0 slice-done.1
  24.3 0.0 copy-start.4
  24.3 0.0 copy-start.1
  24.3 0.0 copy-start.2
  24.3 1.1 fusion.12
  25.4 8.2 %all_gather.16 = bf16[128,2048]{1,0:T(8,128)(2,1)S(1)} all-gather(bf16[128,1024]{1,0:T(8,128)(2,1)S(1)} %fusion.12), channel_id=1, replica_groups=mesh['dp'=2,'expert'=4,'mp'=4] {'dp'}, dimensions={1}, use_global_device_ids=true | all-gather | bytes 786432 | tf_op jit(solution)/shard_map/all_gather | solution.py:24
  33.6 0.0 copy-done.4
  33.6 0.6 dynamic-slice
  34.9 0.2 dynamic-update-slice
  35.1 4.9 %all-reduce = f32[128]{0:T(128)S(1)} all-reduce(f32[128]{0:T(128)S(1)} %dynamic-update-slice), channel_id=1, replica_groups=mesh['dp'=2,'expert'=4,'mp'=4] {'dp'}, use_global_device_ids=true, to_apply=%add | all-reduce | flops 128 | bytes 1024
  40.0 4.7 %fusion.6 = f32[128,1536]{1,0:T(8,128)} fusion(bf16[128,2048]{1,0:T(8,128)(2,1)S(1)} %all_gather.16, bf16[1,1,2048,1536]{3,2,1,0:T(8,128)(2,1)} %param.15, f32[128]{0:T(128)S(1)} %all-reduce), kind=kOutput, calls=%fused_computation.6 | convolution fusion | flops 805502976 | bytes 7602688 | tf_op jit(solution)/shard_map/dot_general | solution.py:25
  44.7 0.0 all-reduce.3.cloned.1.call-update
  44.7 0.0 reduce-scatter.2.cloned.1.call-start
  44.8 0.1 dynamic_slice.7
  44.9 93.2 %all-reduce.3.cloned.1.call-done = f32[128,1536]{1,0:T(8,128)} async-done(((f32[128,1536]{1,0:T(8,128)}), f32[128,1536]{1,0:T(8,128)}) %all-reduce.3.cloned.1.call-update) | async-done | bytes 786448 | tf_op jit(solution)/shard_map/psum | solution.py:26
  138.1 1.9 add_convert_fusion
  140.0 4.9 %fusion.15 = f32[128,2048]{1,0:T(8,128)} fusion(bf16[1536,2048]{1,0:T(8,128)(2,1)} %param.17, bf16[128,1536]{1,0:T(8,128)(2,1)} %add_convert_fusion, f32[1536]{0:T(1024)S(1)} %dynamic_slice.7), kind=kOutput, calls=%fused_computation.15 | convolution fusion | flops 805896192 | bytes 7739392 | tf_op jit(solution)/shard_map/dot_general | solution.py:35
  144.9 0.0 reduce-scatter.2.cloned.1.call-update
  145.0 3.5 %all-to-all-start = ((bf16[2,64,1536]{2,1,0:T(8,128)(2,1)}), bf16[2,64,1536]{2,1,0:T(8,128)(2,1)S(1)}, u32[]{:S(2)}, u32[]{:S(2)}) async-start(bf16[2,64,1536]{2,1,0:T(8,128)(2,1)} %bitcast.4), calls=%async_computation | async-start | bytes 786432 | tf_op jit(solution)/shard_map/all_to_all | solution.py:31
  148.5 10.2 %all-to-all-done = bf16[2,64,1536]{2,1,0:T(8,128)(2,1)S(1)} async-done(((bf16[2,64,1536]{2,1,0:T(8,128)(2,1)}), bf16[2,64,1536]{2,1,0:T(8,128)(2,1)S(1)}, u32[]{:S(2)}, u32[]{:S(2)}) %all-to-all-start) | async-done | bytes 393248 | tf_op jit(solution)/shard_map/all_to_all | solution.py:31
  158.6 0.8 copy.16
  159.4 0.2 multiply_reduce_fusion
  159.6 7.2 %reduce-scatter.2.cloned.1.call-done = f32[64,2048]{1,0:T(8,128)} async-done(((f32[128,2048]{1,0:T(8,128)}), f32[64,2048]{1,0:T(8,128)}) %reduce-scatter.2.cloned.1.call-update) | async-done | bytes 524304 | tf_op jit(solution)/shard_map/reduce_scatter | solution.py:36
  166.8 1.2 multiply_reduce_fusion.1
  168.0 1.4 exponential_reduce_fusion
  169.4 30.6 %all-gather.1 = f32[16,3,64]{2,1,0:T(4,128)S(1)} all-gather(f32[1,3,64]{2,1,0:T(4,128)S(1)} %maximum_bitcast_fusion), channel_id=2, replica_groups=mesh['dp'=2,'expert'=4,'mp'=4] {'expert','mp'}, dimensions={0}, use_global_device_ids=true | all-gather | bytes 13056 | tf_op jit(solution)/shard_map/all_gather | solution.py:45
  200.1 0.5 log_subtract_fusion
  (15 shorter events, 0.1 us)
Async XLA Ops:
  7.2 130.9 %all-reduce.3.cloned.1.call-start = ((), (), s32[]{:S(2)}) async-start(), calls=%async_computation.2 | async-start | bytes 1572864 | tf_op jit(solution)/shard_map/psum | solution.py:26
  7.2 17.0 %slice-start = ((s8[6291456]{0:T(1024)(128)(4,1)}), s8[4194304]{0:T(1024)(128)(4,1)S(1)}, s32[]{:S(2)}) async-start(s8[6291456]{0:T(1024)(128)(4,1)} %bitcast.41), calls=%async_computation.4 | async-start | bytes 8388608
  20.3 3.9 %slice-start.1 = ((s8[6291456]{0:T(1024)(128)(4,1)}), s8[2097152]{0:T(1024)(128)(4,1)S(1)}, s32[]{:S(2)}) async-start(s8[6291456]{0:T(1024)(128)(4,1)} %bitcast.41), calls=%async_computation.5 | async-start | bytes 4194304
  24.3 9.3 %copy-start.4 = (u32[32]{0:T(128)S(1)}, u32[32]{0:T(128)}, u32[]{:S(2)}) copy-start(u32[32]{0:T(128)} %constant.40) | copy-start | bytes 388
  24.3 10.5 %copy-start.1 = (f32[64,2]{0,1:T(2,128)S(1)}, f32[64,2]{0,1:T(2,128)}, u32[]{:S(2)}) copy-start(f32[64,2]{0,1:T(2,128)} %param.11) | copy-start | bytes 1540
  24.3 10.5 %copy-start.2 = (s32[64,2]{0,1:T(2,128)S(1)}, s32[64,2]{0,1:T(2,128)}, u32[]{:S(2)}) copy-start(s32[64,2]{0,1:T(2,128)} %param.10) | copy-start | bytes 1540
  40.0 4.8 %copy-start = (f32[3072]{0:T(1024)S(1)}, f32[3072]{0:T(1024)}, u32[]{:S(2)}) copy-start(f32[3072]{0:T(1024)} %param.16) | copy-start | bytes 36868
  44.7 122.0 %reduce-scatter.2.cloned.1.call-start = ((), (), s32[]{:S(2)}) async-start(), calls=%async_computation.3 | async-start | bytes 1572864 | tf_op jit(solution)/shard_map/reduce_scatter | solution.py:36
  44.9 123.1 %copy-start.3 = (s32[64]{0:T(128)S(1)}, s32[64]{0:T(128)}, u32[]{:S(2)}) copy-start(s32[64]{0:T(128)} %param.12) | copy-start | bytes 772
  145.0 13.7 %all-to-all-start = ((bf16[2,64,1536]{2,1,0:T(8,128)(2,1)}), bf16[2,64,1536]{2,1,0:T(8,128)(2,1)S(1)}, u32[]{:S(2)}, u32[]{:S(2)}) async-start(bf16[2,64,1536]{2,1,0:T(8,128)(2,1)} %bitcast.4), calls=%async_computation | async-start | bytes 786432 | tf_op jit(solution)/shard_map/all_to_all | solution.py:31
Sparse Core Ops, SparseCore 0:
  44.9 93.1 all-reduce.2
  145.1 21.6 reduce-scatter.1
where the time goes:
time: 208 us; the launch traced here: 207 us
  waiting for transfers between devices  111 us (53%)
  blocking collectives  56.8 us (27%)
  between operations  14.9 us (7%)
  matrix products  14.6 us (7%)
  other arithmetic  5.39 us (3%)
  starting transfers between devices  3.56 us (2%)
    psum x1, waiting for transfers between devices, per_device(): summed = lax.psum(part, ('expert', 'mp'))  93.2 us
    all_gather x1, blocking collectives, per_device(): lax.all_gather(jnp.stack([top, total, target_local]), ('expert', 'mp'))  30.6 us
    all_gather x1, blocking collectives, per_device(): all_tokens = lax.all_gather(tokens, 'dp', axis=0, tiled=True)  13.1 us
    all_to_all x1, waiting for transfers between devices, per_device(): lax.all_to_all(mixed_part, 'dp', split_axis=0, concat_axis=1, tiled=True)  10.2 us
    all_gather x1, blocking collectives, per_device(): hidden = lax.all_gather(hidden, 'dp', axis=1, tiled=True)  8.17 us
    reduce_scatter x1, waiting for transfers between devices, per_device(): lax.psum_scatter(logits_part, 'dp', scatter_dimension=0, tiled=True)  7.19 us
    unnamed x1, blocking collectives  4.92 us
    dot_general x1, matrix products, per_device(): logits_part = jnp.dot(gained, lens_head, preferred_element_type=f32)  4.91 us
  transfers between devices with their start and end apart: 3, of which 3 were waited for; matrix products, arithmetic and copies ran while one was open for 1% of the time, Pallas kernels for 0%

commit v1 on v0

--- a/solution.py
+++ b/solution.py
@@ -23,7 +23,7 @@
     hidden = (jax.nn.silu(gate_part) * up_part).astype(bf16)
     hidden = lax.all_gather(hidden, "dp", axis=1, tiled=True)
     part = jnp.dot(hidden, down_mat, preferred_element_type=f32) * all_weights[:, None]
-    summed = lax.psum(part, ("expert", "mp"))
+    summed = jnp.sum(lax.all_gather(part, ("expert", "mp")), axis=0)
     first = lax.axis_index("dp") * own_feats
     own_tokens = lax.dynamic_slice_in_dim(all_tokens, first, own_feats, axis=1)
     own_gain = lax.dynamic_slice_in_dim(norm_gain, first, own_feats, axis=0)

time: 208 us -> 222 us (1.067)
  waiting for transfers between devices: 111 us -> 120 us
  other arithmetic: 5.39 us -> 10.1 us
    all_gather x0 -> x1, waiting for transfers between devices: none -> 102 us  [per_device(): summed = jnp.sum(lax.all_gather(part, ('expert', 'mp')), axis=0)]
    psum x1 -> x0, waiting for transfers between devices: 93.2 us -> none  [per_device(): summed = lax.psum(part, ('expert', 'mp'))]
    reduce_sum x0 -> x1, other arithmetic: none -> 5.88 us  [per_device(): summed = jnp.sum(lax.all_gather(part, ('expert', 'mp')), axis=0)]
  transfers between devices with their start and end apart: 3 -> 3, of which waited for: 3 -> 3; matrix products, arithmetic and copies ran while one was open for 1% -> 0% of each run, Pallas kernels for 0% -> 0%
where the time goes in v1:
time: 222 us; the launch traced here: 221 us
  waiting for transfers between devices  120 us (54%)
  blocking collectives  56.1 us (25%)
  between operations  14.9 us (7%)
  matrix products  14.6 us (7%)
  other arithmetic  10.1 us (5%)
  starting transfers between devices  3.56 us (2%)
    all_gather x1, waiting for transfers between devices, per_device(): summed = jnp.sum(lax.all_gather(part, ('expert', 'mp')), axis=0)  102 us
    all_gather x1, blocking collectives, per_device(): lax.all_gather(jnp.stack([top, total, target_local]), ('expert', 'mp'))  29.9 us
    all_gather x1, blocking collectives, per_device(): all_tokens = lax.all_gather(tokens, 'dp', axis=0, tiled=True)  13.1 us
    all_to_all x1, waiting for transfers between devices, per_device(): lax.all_to_all(mixed_part, 'dp', split_axis=0, concat_axis=1, tiled=True)  11.5 us
    all_gather x1, blocking collectives, per_device(): hidden = lax.all_gather(hidden, 'dp', axis=1, tiled=True)  8.17 us
    reduce_scatter x1, waiting for transfers between devices, per_device(): lax.psum_scatter(logits_part, 'dp', scatter_dimension=0, tiled=True)  6.9 us
    reduce_sum x1, other arithmetic, per_device(): summed = jnp.sum(lax.all_gather(part, ('expert', 'mp')), axis=0)  5.88 us
    unnamed x1, blocking collectives  4.92 us
  transfers between devices with their start and end apart: 3, of which 3 were waited for; matrix products, arithmetic and copies ran while one was open for 0% of the time, Pallas kernels for 0%

profile of v1, /device:TPU:0, one launch (start us, length us, event | category | flops | bytes accessed | tf_op | source)
XLA Modules:
  0.0 221.4 jit_solution(6077024228306911753)
XLA Ops:
  7.2 0.0 all-gather.5.cloned.1.call-start
  7.2 0.0 slice-start
  7.2 13.1 %all_gather.21 = bf16[128,3072]{1,0:T(8,128)(2,1)S(1)} all-gather(bf16[64,3072]{1,0:T(8,128)(2,1)} %param.9), channel_id=1, replica_groups=mesh['dp'=2,'expert'=4,'mp'=4] {'dp'}, dimensions={0}, use_global_device_ids=true | all-gather | bytes 1179648 | tf_op jit(solution)/shard_map/all_gather | solution.py:19
  20.3 3.9 %fusion.4 = f32[128,1024]{1,0:T(8,128)S(1)} fusion(bf16[128,3072]{1,0:T(8,128)(2,1)S(1)} %all_gather.21, bf16[1,3072,1,1024]{3,1,2,0:T(8,128)(2,1)} %param.13), kind=kOutput, calls=%fused_computation.4 | convolution fusion | flops 805306368 | bytes 7602176 | tf_op jit(solution)/shard_map/dot_general | solution.py:21
  24.2 0.0 slice-done
  24.3 0.0 copy-start.4
  24.3 0.0 copy-start.1
  24.3 0.0 copy-start.2
  24.3 1.1 fusion.12
  25.4 8.2 %all_gather.22 = bf16[128,2048]{1,0:T(8,128)(2,1)S(1)} all-gather(bf16[128,1024]{1,0:T(8,128)(2,1)S(1)} %fusion.12), channel_id=1, replica_groups=mesh['dp'=2,'expert'=4,'mp'=4] {'dp'}, dimensions={1}, use_global_device_ids=true | all-gather | bytes 786432 | tf_op jit(solution)/shard_map/all_gather | solution.py:24
  33.6 0.6 dynamic-slice
  34.9 0.2 dynamic-update-slice
  35.1 4.9 %all-reduce = f32[128]{0:T(128)S(1)} all-reduce(f32[128]{0:T(128)S(1)} %dynamic-update-slice), channel_id=1, replica_groups=mesh['dp'=2,'expert'=4,'mp'=4] {'dp'}, use_global_device_ids=true, to_apply=%add | all-reduce | flops 128 | bytes 1024
  40.0 4.7 %fusion.6 = f32[128,1536]{1,0:T(8,128)} fusion(bf16[128,2048]{1,0:T(8,128)(2,1)S(1)} %all_gather.22, bf16[1,1,2048,1536]{3,2,1,0:T(8,128)(2,1)} %param.15, f32[128]{0:T(128)S(1)} %all-reduce), kind=kOutput, calls=%fused_computation.6 | convolution fusion | flops 805502976 | bytes 7602688 | tf_op jit(solution)/shard_map/dot_general | solution.py:25
  44.7 0.0 all-gather.5.cloned.1.call-update
  44.8 0.0 reduce-scatter.2.cloned.1.call-start
  44.8 0.1 dynamic_slice.7
  44.9 102.0 %all-gather.5.cloned.1.call-done = f32[2048,1536]{1,0:T(8,128)} async-done(((f32[128,1536]{1,0:T(8,128)}), f32[2048,1536]{1,0:T(8,128)}) %all-gather.5.cloned.1.call-update) | async-done | bytes 12582928 | tf_op jit(solution)/shard_map/all_gather | solution.py:26
  146.9 5.9 %reduce_sum.64 = f32[128,1536]{1,0:T(8,128)S(1)} reduce(f32[16,128,1536]{2,1,0:T(8,128)} %bitcast.35, f32[]{:T(128)} %constant.29.clone.1), dimensions={0}, to_apply=%region_1.2 | reduce | flops 2949120 | bytes 13369348 | tf_op jit(solution)/shard_map/reduce_sum | solution.py:26
  152.7 0.0 copy-start.3
  152.8 0.8 add_convert_fusion
  153.6 4.9 %fusion.15 = f32[128,2048]{1,0:T(8,128)} fusion(bf16[1536,2048]{1,0:T(8,128)(2,1)} %param.17, bf16[128,1536]{1,0:T(8,128)(2,1)} %add_convert_fusion, f32[1536]{0:T(1024)S(1)} %dynamic_slice.7), kind=kOutput, calls=%fused_computation.15 | convolution fusion | flops 805896192 | bytes 7739392 | tf_op jit(solution)/shard_map/dot_general | solution.py:35
  158.5 0.0 reduce-scatter.2.cloned.1.call-update
  158.5 3.5 %all-to-all-start = ((bf16[2,64,1536]{2,1,0:T(8,128)(2,1)}), bf16[2,64,1536]{2,1,0:T(8,128)(2,1)S(1)}, u32[]{:S(2)}, u32[]{:S(2)}) async-start(bf16[2,64,1536]{2,1,0:T(8,128)(2,1)} %bitcast.5), calls=%async_computation | async-start | bytes 786432 | tf_op jit(solution)/shard_map/all_to_all | solution.py:31
  162.0 11.5 %all-to-all-done = bf16[2,64,1536]{2,1,0:T(8,128)(2,1)S(1)} async-done(((bf16[2,64,1536]{2,1,0:T(8,128)(2,1)}), bf16[2,64,1536]{2,1,0:T(8,128)(2,1)S(1)}, u32[]{:S(2)}, u32[]{:S(2)}) %all-to-all-start) | async-done | bytes 393248 | tf_op jit(solution)/shard_map/all_to_all | solution.py:31
  173.5 0.8 copy.17
  174.3 0.2 multiply_reduce_fusion
  174.5 6.9 %reduce-scatter.2.cloned.1.call-done = f32[64,2048]{1,0:T(8,128)} async-done(((f32[128,2048]{1,0:T(8,128)}), f32[64,2048]{1,0:T(8,128)}) %reduce-scatter.2.cloned.1.call-update) | async-done | bytes 524304 | tf_op jit(solution)/shard_map/reduce_scatter | solution.py:36
  181.4 1.2 multiply_reduce_fusion.1
  182.7 1.4 exponential_reduce_fusion
  184.1 29.9 %all-gather.2 = f32[16,3,64]{2,1,0:T(4,128)S(1)} all-gather(f32[1,3,64]{2,1,0:T(4,128)S(1)} %maximum_bitcast_fusion), channel_id=3, replica_groups=mesh['dp'=2,'expert'=4,'mp'=4] {'expert','mp'}, dimensions={0}, use_global_device_ids=true | all-gather | bytes 13056 | tf_op jit(solution)/shard_map/all_gather | solution.py:45
  214.1 0.5 log_subtract_fusion
  (16 shorter events, 0.1 us)
Async XLA Ops:
  7.2 139.7 %all-gather.5.cloned.1.call-start = ((), (), s32[]{:S(2)}) async-start(), calls=%async_computation.3 | async-start | bytes 13369344 | tf_op jit(solution)/shard_map/all_gather | solution.py:26
  7.2 17.0 %slice-start = ((s8[6291456]{0:T(1024)(128)(4,1)}), s8[4194304]{0:T(1024)(128)(4,1)S(1)}, s32[]{:S(2)}) async-start(s8[6291456]{0:T(1024)(128)(4,1)} %bitcast.43), calls=%async_computation.4 | async-start | bytes 8388608
  20.3 3.9 %slice-start.1 = ((s8[6291456]{0:T(1024)(128)(4,1)}), s8[2097152]{0:T(1024)(128)(4,1)S(1)}, s32[]{:S(2)}) async-start(s8[6291456]{0:T(1024)(128)(4,1)} %bitcast.43), calls=%async_computation.5 | async-start | bytes 4194304
  24.3 9.3 %copy-start.4 = (u32[32]{0:T(128)S(1)}, u32[32]{0:T(128)}, u32[]{:S(2)}) copy-start(u32[32]{0:T(128)} %constant.40) | copy-start | bytes 388
  24.3 10.5 %copy-start.1 = (f32[64,2]{0,1:T(2,128)S(1)}, f32[64,2]{0,1:T(2,128)}, u32[]{:S(2)}) copy-start(f32[64,2]{0,1:T(2,128)} %param.11) | copy-start | bytes 1540
  24.3 10.5 %copy-start.2 = (s32[64,2]{0,1:T(2,128)S(1)}, s32[64,2]{0,1:T(2,128)}, u32[]{:S(2)}) copy-start(s32[64,2]{0,1:T(2,128)} %param.10) | copy-start | bytes 1540
  40.0 4.8 %copy-start = (f32[3072]{0:T(1024)S(1)}, f32[3072]{0:T(1024)}, u32[]{:S(2)}) copy-start(f32[3072]{0:T(1024)} %param.16) | copy-start | bytes 36868
  44.8 136.6 %reduce-scatter.2.cloned.1.call-start = ((), (), s32[]{:S(2)}) async-start(), calls=%async_computation.2 | async-start | bytes 1572864 | tf_op jit(solution)/shard_map/reduce_scatter | solution.py:36
  152.7 29.9 %copy-start.3 = (s32[64]{0:T(128)S(1)}, s32[64]{0:T(128)}, u32[]{:S(2)}) copy-start(s32[64]{0:T(128)} %param.12) | copy-start | bytes 772
  158.5 15.0 %all-to-all-start = ((bf16[2,64,1536]{2,1,0:T(8,128)(2,1)}), bf16[2,64,1536]{2,1,0:T(8,128)(2,1)S(1)}, u32[]{:S(2)}, u32[]{:S(2)}) async-start(bf16[2,64,1536]{2,1,0:T(8,128)(2,1)} %bitcast.5), calls=%async_computation | async-start | bytes 786432 | tf_op jit(solution)/shard_map/all_to_all | solution.py:31
Sparse Core Ops, SparseCore 0:
  44.9 101.9 all-gather.4
  158.6 22.7 reduce-scatter.1
